TPU v7x, 32 devices: a whole 2x2x4 slice. The times are simulated.
32 devices in a mesh: tm: 16 (over z, x, core), fsdp: 2 (over y).
Axes of the slice: x: 2, y: 2, z: 4, core: 2. Of those that a mesh axis runs over, the one named last changes fastest.
Arguments:
- frames: bfloat16 [2, 2, 24576, 512], P(None, 'fsdp', 'tm'), may hold values from -6 to 6
- conditioning: bfloat16 [2, 2, 24576, 512], P(None, 'fsdp', 'tm'), may hold values from -6 to 6
- lengths: int32 [2, 2, 30], P(None, 'fsdp'), may hold values from 1 to 1600, 24576 in all within a row
- steps: int32 [2, 2, 30], P(None, 'fsdp'), may hold values from 0 to 999
- prompt: bfloat16 [2, 2, 256, 512], P(None, 'fsdp', 'tm'), may hold values from -6 to 6
- queries: float32 [32, 512], P('fsdp'), may hold values from -6 to 6
- w_step: float32 [512, 1024], P('fsdp'), may hold values from -0.25 to 0.25
- w_cond: float32 [512, 1024], P('fsdp'), may hold values from -0.25 to 0.25
- w_conv: float32 [3, 512, 1024], P(None, 'fsdp'), may hold values from -0.15625 to 0.15625
- w_query: float32 [512, 512], P('fsdp'), may hold values from -0.25 to 0.25
- w_key: float32 [512, 512], P('fsdp'), may hold values from -0.25 to 0.25
- w_value: float32 [512, 512], P('fsdp'), may hold values from -0.25 to 0.25
- w_out: float32 [512, 512], P('fsdp'), may hold values from -2 to 2
- w_film: float32 [512, 1024], P('fsdp'), may hold values from -2 to 2
- w_proj: float32 [512, 1024], P('fsdp'), may hold values from -0.25 to 0.25
- grad_res: bfloat16 [2, 2, 24576, 512], P(None, 'fsdp', 'tm'), may hold values from -6 to 6
- grad_skip: bfloat16 [2, 2, 24576, 512], P(None, 'fsdp', 'tm'), may hold values from -6 to 6
Outputs:
- res_out: bfloat16 [2, 2, 24576, 512], P(None, 'fsdp', 'tm')
- skip_out: bfloat16 [2, 2, 24576, 512], P(None, 'fsdp', 'tm')
- grad_frames: float32 [2, 2, 24576, 512], P(None, 'fsdp', 'tm')
- grad_prompt: float32 [2, 2, 256, 512], P(None, 'fsdp', 'tm')
- grad_queries: float32 [32, 512], P('fsdp')
- grad_step: float32 [512, 1024], P('fsdp')
- grad_cond: float32 [512, 1024], P('fsdp')
- grad_conv: float32 [3, 512, 1024], P(None, 'fsdp')
- grad_query: float32 [512, 512], P('fsdp')
- grad_key: float32 [512, 512], P('fsdp')
- grad_value: float32 [512, 512], P('fsdp')
- grad_out: float32 [512, 512], P('fsdp')
- grad_film: float32 [512, 1024], P('fsdp')
- grad_proj: float32 [512, 1024], P('fsdp')
Inputs may be any that keep to these rules, and one draw needn't show every extreme that they name: Each pack's 30 lengths sum to its 24576 frames; the last entry is the padding at the pack's end; the longest entry is exactly 1600.
All inputs are finite; a program needn't handle non-finite values.
Results may differ from a plain program's by a relative error of at most 0.0085.
The roundings to bfloat16 on the way count: a program that leaves them out, or rounds other values in their place, can miss the bound.
Values may be sent and summed in bfloat16 or wider, within the bound.
No kernel may reach another device: no remote copies, remote signals or barrier semaphores. Data moves between devices by JAX's collectives and lax.ppermute only.
A program may use at most 104 MiB of HBM per device.

v0:
```python
import math
import jax
import jax.numpy as jnp
from jax import lax
from jax.sharding import PartitionSpec as P

HEADS = 8
QUERIES = 32
DILATION = 16
MICRO = 2
PRECISE = lax.Precision.HIGHEST
SQRT_HALF = 0.7071067811865476


def padded(block, sides, width):
    for axis, dim in sides:
        count = lax.axis_size(axis)
        forward = [(i, i + 1) for i in range(count - 1)]
        backward = [(target, source) for source, target in forward]
        low = lax.ppermute(
            lax.slice_in_dim(block, block.shape[dim] - width, None, axis=dim), axis, forward
        )
        high = lax.ppermute(lax.slice_in_dim(block, 0, width, axis=dim), axis, backward)
        block = jnp.concatenate([low, block, high], axis=dim)
    return block


def joined_2(part, axis, combine):
    gathered = jax.tree.map(lambda a: lax.all_gather(a, axis), part)

    def take(source):
        return jax.tree.map(lambda a: lax.dynamic_index_in_dim(a, source, 0, False), gathered)

    return lax.fori_loop(
        1, lax.axis_size(axis), lambda source, state: combine(state, take(source)), take(0)
    )


def contract_rows(left, right, precision=None):
    return lax.dot_general(
        left,
        right,
        (((0,), (0,)), ((), ())),
        precision=precision,
        preferred_element_type=jnp.float32,
    )


def contract_cols(left, right, precision=None):
    return lax.dot_general(
        left,
        right,
        (((1,), (1,)), ((), ())),
        precision=precision,
        preferred_element_type=jnp.float32,
    )


def softmax_join(earlier, later):
    joined = jnp.maximum(earlier[0], later[0])
    return (
        joined,
        earlier[1] * jnp.exp(earlier[0] - joined) + later[1] * jnp.exp(later[0] - joined),
    )


def step_embedding(pack_steps, width):
    half_width = width // 2
    freqs = jnp.exp(jnp.arange(half_width).astype(jnp.float32) * (-math.log(10000.0) / half_width))
    angles = pack_steps.astype(jnp.float32)[:, None] * freqs[None, :]
    return jnp.concatenate([jnp.sin(angles), jnp.cos(angles)], axis=1)


def per_device(
    frames,
    conditioning,
    lengths,
    steps,
    prompt,
    queries,
    w_step,
    w_cond,
    w_conv,
    w_query,
    w_key,
    w_value,
    w_out,
    w_film,
    w_proj,
    grad_res,
    grad_skip,
):
    frames_dev = frames.shape[2]
    width = frames.shape[3]
    prompt_rows_dev = prompt.shape[2]
    head_size = width // HEADS
    score_scale = 1.0 / math.sqrt(head_size)
    bf16 = jnp.bfloat16
    f32 = jnp.float32
    shard_q = queries.astype(bf16)
    shard_step = w_step.astype(bf16)
    shard_cond = w_cond.astype(bf16)
    shard_conv = w_conv.astype(bf16)
    shard_query = w_query.astype(bf16)
    shard_key = w_key.astype(bf16)
    shard_value = w_value.astype(bf16)
    shard_out = w_out.astype(bf16)
    shard_film = w_film.astype(bf16)
    shard_proj = w_proj.astype(bf16)
    tm_index = lax.axis_index("tm")
    first_rank = (tm_index == 0).astype(f32)
    acc_q = jnp.zeros((QUERIES, width), f32)
    acc_step = jnp.zeros((width, 2 * width), f32)
    acc_cond = jnp.zeros((width, 2 * width), f32)
    acc_conv = jnp.zeros((3 * width, 2 * width), f32)
    acc_query = jnp.zeros((width, width), f32)
    acc_key = jnp.zeros((width, width), f32)
    acc_value = jnp.zeros((width, width), f32)
    acc_out = jnp.zeros((width, width), f32)
    acc_film = jnp.zeros((width, 2 * width), f32)
    acc_proj = jnp.zeros((width, 2 * width), f32)
    res_list, skip_list, frame_list, prompt_list = ([], [], [], [])
    for micro_index in range(MICRO):
        gathered = (
            lax.all_gather(shard_q, "fsdp", axis=0, tiled=True),
            lax.all_gather(shard_step, "fsdp", axis=0, tiled=True),
            lax.all_gather(shard_cond, "fsdp", axis=0, tiled=True),
            lax.all_gather(shard_conv, "fsdp", axis=1, tiled=True),
            lax.all_gather(shard_query, "fsdp", axis=0, tiled=True),
            lax.all_gather(shard_key, "fsdp", axis=0, tiled=True),
            lax.all_gather(shard_value, "fsdp", axis=0, tiled=True),
            lax.all_gather(shard_out, "fsdp", axis=0, tiled=True),
            lax.all_gather(shard_film, "fsdp", axis=0, tiled=True),
            lax.all_gather(shard_proj, "fsdp", axis=0, tiled=True),
        )
        (
            full_q,
            full_step,
            full_cond,
            full_conv,
            full_query,
            full_key,
            full_value,
            full_out,
            full_film,
            full_proj,
        ) = gathered
        conv_flat = full_conv.reshape(3 * width, 2 * width)
        frame_rows = frames[micro_index, 0].astype(f32)
        cond_rows = conditioning[micro_index, 0]
        pack_lengths = lengths[micro_index, 0]
        utter_count = pack_lengths.shape[0]
        utter_ends = jnp.cumsum(pack_lengths)
        positions = tm_index * frames_dev - DILATION + jnp.arange(frames_dev + 2 * DILATION)
        seg_ext = jnp.sum((positions[:, None] >= utter_ends[None, :]).astype(jnp.int32), axis=1)
        segment = seg_ext[DILATION : DILATION + frames_dev]
        live_mask = (segment < utter_count - 1).astype(f32)
        same_taps = [
            seg_ext[tap * DILATION : tap * DILATION + frames_dev] == segment for tap in range(3)
        ]
        one_hot = (segment[:, None] == jnp.arange(utter_count)[None, :]).astype(f32)
        step_low = step_embedding(steps[micro_index, 0], width).astype(bf16)
        step_film = jnp.dot(step_low, full_step, preferred_element_type=f32)
        film_first = jnp.dot(one_hot, step_film, precision=PRECISE) + jnp.dot(
            cond_rows, full_cond, preferred_element_type=f32
        )
        gain_first = film_first[:, :width]
        hidden_low = (frame_rows * (1.0 + gain_first) + film_first[:, width:]).astype(bf16)
        extended = padded(hidden_low, (("tm", 0),), DILATION)
        stacked = jnp.concatenate(
            [
                extended[tap * DILATION : tap * DILATION + frames_dev]
                * same_taps[tap][:, None].astype(bf16)
                for tap in range(3)
            ],
            axis=1,
        )
        conv_out = jnp.dot(stacked, conv_flat, preferred_element_type=f32)
        tanh_part = jnp.tanh(conv_out[:, :width])
        sigm_part = jax.nn.sigmoid(conv_out[:, width:])
        activated = tanh_part * sigm_part
        prompt_rows = prompt[micro_index, 0]
        query_low = jnp.dot(full_q, full_query, preferred_element_type=f32).astype(bf16)
        key_low = jnp.dot(prompt_rows, full_key, preferred_element_type=f32).astype(bf16)
        value_low = jnp.dot(prompt_rows, full_value, preferred_element_type=f32).astype(bf16)
        query_heads = query_low.reshape(QUERIES, HEADS, head_size)
        key_heads = key_low.reshape(prompt_rows_dev, HEADS, head_size)
        value_heads = value_low.reshape(prompt_rows_dev, HEADS, head_size)
        scores = (
            jnp.einsum("qhd,khd->hqk", query_heads, key_heads, preferred_element_type=f32)
            * score_scale
        )
        local_top = jnp.max(scores, axis=-1)
        local_total = jnp.sum(jnp.exp(scores - local_top[..., None]), axis=-1)
        score_top, score_total = joined_2((local_top, local_total), "tm", softmax_join)
        probs = jnp.exp(scores - score_top[..., None]) / score_total[..., None]
        probs_low = probs.astype(bf16)
        context_part = jnp.einsum(
            "hqk,khd->qhd", probs_low, value_heads, preferred_element_type=f32
        ).reshape(QUERIES, width)
        context = lax.psum(context_part, "tm")
        context_low = context.astype(bf16)
        projected = jnp.dot(context_low, full_out, preferred_element_type=f32)
        summary_low = jnp.mean(projected, axis=0).astype(bf16)
        film_second = jnp.dot(summary_low[None, :], full_film, preferred_element_type=f32)[0]
        gain_second = film_second[:width]
        gated_low = (activated * (1.0 + gain_second) + film_second[width:]).astype(bf16)
        branch_out = jnp.dot(gated_low, full_proj, preferred_element_type=f32)
        res_list.append(
            ((frame_rows + branch_out[:, :width]) * SQRT_HALF * live_mask[:, None]).astype(bf16)
        )
        skip_list.append((branch_out[:, width:] * live_mask[:, None]).astype(bf16))
        res_cot = grad_res[micro_index, 0].astype(f32) * SQRT_HALF * live_mask[:, None]
        skip_cot = grad_skip[micro_index, 0].astype(f32) * live_mask[:, None]
        branch_cot = jnp.concatenate([res_cot, skip_cot], axis=1).astype(bf16)
        acc_proj = acc_proj + contract_rows(gated_low, branch_cot)
        gated_cot = contract_cols(branch_cot, full_proj)
        film_local = jnp.concatenate(
            [jnp.sum(gated_cot * activated, axis=0), jnp.sum(gated_cot, axis=0)]
        )
        film_cot = lax.psum(film_local, "tm")
        summary_f32 = summary_low.astype(f32)
        acc_film = acc_film + first_rank * (summary_f32[:, None] * film_cot[None, :])
        summary_cot = jnp.dot(full_film.astype(f32), film_cot, precision=PRECISE) / QUERIES
        context_total = jnp.sum(context_low.astype(f32), axis=0)
        acc_out = acc_out + first_rank * (context_total[:, None] * summary_cot[None, :])
        context_cot_row = jnp.dot(full_out.astype(f32), summary_cot, precision=PRECISE)
        context_cot = jnp.broadcast_to(context_cot_row[None, :], (QUERIES, width)).astype(bf16)
        context_cot_heads = context_cot.reshape(QUERIES, HEADS, head_size)
        prob_cot = jnp.einsum(
            "qhd,khd->hqk", context_cot_heads, value_heads, preferred_element_type=f32
        )
        row_part = jnp.sum(probs * prob_cot, axis=-1)
        row_total = lax.psum(row_part, "tm")
        score_cot = (probs * (prob_cot - row_total[..., None])).astype(bf16)
        query_cot = (
            jnp.einsum("hqk,khd->qhd", score_cot, key_heads, preferred_element_type=f32)
            * score_scale
        ).reshape(QUERIES, width)
        key_cot = (
            (
                jnp.einsum("hqk,qhd->khd", score_cot, query_heads, preferred_element_type=f32)
                * score_scale
            )
            .astype(bf16)
            .reshape(prompt_rows_dev, width)
        )
        value_cot = (
            jnp.einsum("hqk,qhd->khd", probs_low, context_cot_heads, preferred_element_type=f32)
            .astype(bf16)
            .reshape(prompt_rows_dev, width)
        )
        prompt_list.append(contract_cols(key_cot, full_key) + contract_cols(value_cot, full_value))
        acc_key = acc_key + contract_rows(prompt_rows, key_cot)
        acc_value = acc_value + contract_rows(prompt_rows, value_cot)
        acc_query = acc_query + contract_rows(full_q.astype(f32), query_cot, PRECISE)
        acc_q = acc_q + contract_cols(query_cot, full_query.astype(f32), PRECISE)
        act_cot = gated_cot * (1.0 + gain_second)
        conv_cot = jnp.concatenate(
            [
                act_cot * sigm_part * (1.0 - tanh_part * tanh_part),
                act_cot * tanh_part * sigm_part * (1.0 - sigm_part),
            ],
            axis=1,
        ).astype(bf16)
        acc_conv = acc_conv + contract_rows(stacked, conv_cot)
        cot_extended = padded(conv_cot, (("tm", 0),), DILATION)
        back_taps = jnp.stack(
            [
                cot_extended[(2 - tap) * DILATION : (2 - tap) * DILATION + frames_dev]
                * same_taps[2 - tap][:, None].astype(bf16)
                for tap in range(3)
            ],
            axis=1,
        )
        hidden_cot = lax.dot_general(
            back_taps, full_conv, (((1, 2), (0, 2)), ((), ())), preferred_element_type=f32
        )
        film_first_cot = jnp.concatenate([hidden_cot * frame_rows, hidden_cot], axis=1).astype(bf16)
        acc_cond = acc_cond + contract_rows(cond_rows, film_first_cot)
        step_film_cot = contract_rows(one_hot, film_first_cot.astype(f32), PRECISE)
        acc_step = acc_step + contract_rows(step_low.astype(f32), step_film_cot, PRECISE)
        frame_list.append(res_cot + hidden_cot * (1.0 + gain_first))
    acc_conv_taps = acc_conv.reshape(3, width, 2 * width)
    shares = (
        lax.psum_scatter(acc_q, "fsdp", scatter_dimension=0, tiled=True),
        lax.psum_scatter(acc_step, "fsdp", scatter_dimension=0, tiled=True),
        lax.psum_scatter(acc_cond, "fsdp", scatter_dimension=0, tiled=True),
        lax.psum_scatter(acc_conv_taps, "fsdp", scatter_dimension=1, tiled=True),
        lax.psum_scatter(acc_query, "fsdp", scatter_dimension=0, tiled=True),
        lax.psum_scatter(acc_key, "fsdp", scatter_dimension=0, tiled=True),
        lax.psum_scatter(acc_value, "fsdp", scatter_dimension=0, tiled=True),
        lax.psum_scatter(acc_out, "fsdp", scatter_dimension=0, tiled=True),
        lax.psum_scatter(acc_film, "fsdp", scatter_dimension=0, tiled=True),
        lax.psum_scatter(acc_proj, "fsdp", scatter_dimension=0, tiled=True),
    )
    summed = lax.psum(
        (
            shares[0],
            shares[1],
            shares[2],
            shares[3],
            shares[4],
            shares[5],
            shares[6],
            shares[7],
            shares[8],
            shares[9],
        ),
        "tm",
    )
    res_out = jnp.stack(res_list)[:, None]
    skip_out = jnp.stack(skip_list)[:, None]
    grad_frames = jnp.stack(frame_list)[:, None]
    grad_prompt = jnp.stack(prompt_list)[:, None]
    return (
        res_out,
        skip_out,
        grad_frames,
        grad_prompt,
        summed[0],
        summed[1],
        summed[2],
        summed[3],
        summed[4],
        summed[5],
        summed[6],
        summed[7],
        summed[8],
        summed[9],
    )


def solution(mesh):
    in_specs = (
        P(None, "fsdp", "tm", None),
        P(None, "fsdp", "tm", None),
        P(None, "fsdp", None),
        P(None, "fsdp", None),
        P(None, "fsdp", "tm", None),
        P("fsdp", None),
        P("fsdp", None),
        P("fsdp", None),
        P(None, "fsdp", None),
        P("fsdp", None),
        P("fsdp", None),
        P("fsdp", None),
        P("fsdp", None),
        P("fsdp", None),
        P("fsdp", None),
        P(None, "fsdp", "tm", None),
        P(None, "fsdp", "tm", None),
    )
    out_specs = (
        P(None, "fsdp", "tm", None),
        P(None, "fsdp", "tm", None),
        P(None, "fsdp", "tm", None),
        P(None, "fsdp", "tm", None),
        P("fsdp", None),
        P("fsdp", None),
        P("fsdp", None),
        P(None, "fsdp", None),
        P("fsdp", None),
        P("fsdp", None),
        P("fsdp", None),
        P("fsdp", None),
        P("fsdp", None),
        P("fsdp", None),
    )
    return jax.shard_map(
        per_device, mesh=mesh, in_specs=in_specs, out_specs=out_specs, check_vma=False
    )
```

profile of v0, /device:TPU:0, one launch (start us, length us, event | category | flops | bytes accessed | tf_op | source)
XLA Modules:
  0.0 827.9 jit_solution(15819924831970833689)
XLA Ops:
  7.2 2.2 convert_element_type.310
  17.6 15.5 %all_gather.70 = bf16[512,512]{1,0:T(8,128)(2,1)S(1)} all-gather(bf16[256,512]{1,0:T(8,128)(2,1)S(1)} %convert_element_type.320), channel_id=1, replica_groups=mesh['tm'=16,'fsdp'=2] {'fsdp'}, dimensions={0}, use_global_device_ids=true | all-gather | bytes 786432 | tf_op jit(solution)/shard_map/all_gather | solution.py:130
  34.2 10.2 %all_gather.67 = bf16[512,512]{1,0:T(8,128)(2,1)S(1)} all-gather(bf16[256,512]{1,0:T(8,128)(2,1)S(1)} %convert_element_type.315), channel_id=1, replica_groups=mesh['tm'=16,'fsdp'=2] {'fsdp'}, dimensions={0}, use_global_device_ids=true | all-gather | bytes 786432 | tf_op jit(solution)/shard_map/all_gather | solution.py:131
  45.5 4.4 all_gather.68
  49.9 13.5 %all_gather.69 = bf16[512,512]{1,0:T(8,128)(2,1)S(1)} all-gather(bf16[256,512]{1,0:T(8,128)(2,1)S(1)} %convert_element_type.318), channel_id=1, replica_groups=mesh['tm'=16,'fsdp'=2] {'fsdp'}, dimensions={0}, use_global_device_ids=true | all-gather | bytes 786432 | tf_op jit(solution)/shard_map/all_gather | solution.py:129
  64.1 22.6 %all-gather = f32[128,32]{1,0:T(8,128)S(1)} all-gather(f32[8,32]{1,0:T(8,128)S(1)} %get-tuple-element.438), channel_id=2, replica_groups=mesh['tm'=16,'fsdp'=2] {'tm'}, dimensions={0}, use_global_device_ids=true | all-gather | bytes 17408 | tf_op jit(solution)/shard_map/all_gather | solution.py:29
  86.7 17.6 %all-gather.1 = f32[128,32]{1,0:T(8,128)S(1)} all-gather(f32[8,32]{1,0:T(8,128)S(1)} %exponential_reduce_fusion.1), channel_id=3, replica_groups=mesh['tm'=16,'fsdp'=2] {'tm'}, dimensions={0}, use_global_device_ids=true | all-gather | bytes 17408 | tf_op jit(solution)/shard_map/all_gather | solution.py:29
  105.0 18.9 %all-gather.2 = f32[128,32]{1,0:T(8,128)S(1)} all-gather(f32[8,32]{1,0:T(8,128)S(1)} %get-tuple-element.436), channel_id=4, replica_groups=mesh['tm'=16,'fsdp'=2] {'tm'}, dimensions={0}, use_global_device_ids=true | all-gather | bytes 17408 | tf_op jit(solution)/shard_map/all_gather | solution.py:29
  124.0 17.6 %all-gather.3 = f32[128,32]{1,0:T(8,128)S(1)} all-gather(f32[8,32]{1,0:T(8,128)S(1)} %exponential_reduce_fusion), channel_id=5, replica_groups=mesh['tm'=16,'fsdp'=2] {'tm'}, dimensions={0}, use_global_device_ids=true | all-gather | bytes 17408 | tf_op jit(solution)/shard_map/all_gather | solution.py:29
  142.5 11.0 %all_gather.75 = bf16[512,512]{1,0:T(8,128)(2,1)S(1)} all-gather(bf16[256,512]{1,0:T(8,128)(2,1)S(1)} %convert_element_type.324), channel_id=1, replica_groups=mesh['tm'=16,'fsdp'=2] {'fsdp'}, dimensions={0}, use_global_device_ids=true | all-gather | bytes 786432 | tf_op jit(solution)/shard_map/all_gather | solution.py:132
  153.8 3.6 fusion.63
  159.6 6.2 fusion.88
  167.3 5.3 convolution_add_fusion
  175.0 2.9 convolution_add_fusion.1
  183.4 5.1 collective-permute-start
  189.9 3.7 fusion.84
  193.6 3.6 fusion.86
  197.2 9.2 %fusion.78 = f32[1536,1024]{1,0:T(8,128)} fusion(bf16[1536,1024]{1,0:T(8,128)(2,1)} %bitcast.275, bf16[1536,512]{1,0:T(8,128)(2,1)} %get-tuple-element.411, bf16[1536,512]{1,0:T(8,128)(2,1)S(1)} %get-tuple-element.404, bf16[1536,512]{1,0:T(8,128)(2,1)} %get-tuple-element.410), kind=kOutput, calls=%fused_computation.128 | convolution fusion | flops 4845993984 | bytes 14155776 | tf_op jit(solution)/shard_map/dot_general | solution.py:178
  206.5 8.5 %multiply_reduce_fusion.1 = (f32[512]{0:T(512)S(1)}, f32[512]{0:T(512)S(1)}, f32[1536,512]{1,0:T(8,128)}) fusion(f32[1536,1024]{1,0:T(8,128)} %fusion.78, bf16[512,1024]{1,0:T(8,128)(2,1)} %all-gather.18.cloned.1.call-done, bf16[1536,512]{1,0:T(8,128)(2,1)} %get-tuple-element.408, bf16[1536,512]{1,0:T(8,128)(2,1)} %get-tuple-element.406), kind=kOutput, calls=%fused_computation.108 | convolution fusion | flops 1622408192 | bytes 13635584 | tf_op jit(solution)/shard_map/dot_general | solution.py:50
  215.0 5.1 fusion.77
  220.2 3.9 multiply_reduce_fusion
  224.0 32.8 %all-reduce.2 = (f32[1024]{0:T(1024)S(1)}, f32[1024]{0:T(1024)S(1)}) all-reduce(f32[1024]{0:T(1024)S(1)} %pad_maximum_fusion.45, f32[1024]{0:T(1024)S(1)} %pad_maximum_fusion.44), channel_id=1, replica_groups=mesh['tm'=16,'fsdp'=2] {'tm'}, use_global_device_ids=true, to_apply=%region_23.24 | all-reduce | flops 2048 | bytes 16384 | tf_op jit(solution)/shard_map/psum | solution.py:221
  262.8 30.0 %all-reduce.1 = (f32[8,32]{1,0:T(8,128)S(1)}, f32[8,32]{1,0:T(8,128)S(1)}) all-reduce(f32[8,32]{1,0:T(8,128)S(1)} %get-tuple-element.442, f32[8,32]{1,0:T(8,128)S(1)} %get-tuple-element.444), channel_id=1, replica_groups=mesh['tm'=16,'fsdp'=2] {'tm'}, use_global_device_ids=true, to_apply=%region_25.26 | all-reduce | flops 512 | bytes 4096 | tf_op jit(solution)/shard_map/psum | solution.py:234
  303.0 61.7 %all-reduce.8 = (bf16[32,512]{1,0:T(8,128)(2,1)S(1)}, bf16[32,512]{1,0:T(8,128)(2,1)S(1)}, f32[16,512]{1,0:T(8,128)}) all-reduce(f32[32,512]{1,0:T(8,128)S(1)} %reshape.308, f32[32,512]{1,0:T(8,128)S(1)} %reshape.303, f32[16,512]{1,0:T(8,128)} %reduce-scatter.11.cloned.1.call-done), channel_id=1, replica_groups=mesh['tm'=16,'fsdp'=2] {'tm'}, use_global_device_ids=true, to_apply=%region_14.15 | all-reduce | flops 40960 | bytes 262144 | tf_op jit(solution)/shard_map/psum | solution.py:201
  368.0 5.8 multiply_convert_fusion.1
  378.1 3.2 multiply_convert_fusion.3
  382.5 3.2 fusion.95
  388.0 3.0 collective-permute-start.5
  392.9 3.0 collective-permute-start.7
  397.8 6.3 fusion.199
  404.1 10.7 %fusion.39 = (bf16[1536,1,1024]{2,0,1:T(8,128)(2,1)}, bf16[1536,1,1024]{2,0,1:T(8,128)(2,1)}) fusion(bf16[16,1024]{1,0:T(8,128)(2,1)S(1)} %collective-permute-done.6, bf16[1536,512]{1,0:T(8,128)(2,1)S(1)} %copy-done.3, bf16[1536,512]{1,0:T(8,128)(2,1)S(1)} %get-tuple-element.382, bf16[1536]{0:T(1024)(128)(2,1)S(1)} %get-tuple-element.421, ...), kind=kLoop, calls=%fused_computation.56 | loop fusion | flops 25165824 | bytes 9508864 | tf_op jit(solution)/shard_map/stack | solution.py:268
  414.9 9.1 %fusion.43 = (bf16[1536,1,1024]{2,0,1:T(8,128)(2,1)S(1)}, bf16[1536,1,1024]{2,0,1:T(8,128)(2,1)S(1)}) fusion(bf16[16,1024]{1,0:T(8,128)(2,1)S(1)} %collective-permute-done.4, bf16[1536,512]{1,0:T(8,128)(2,1)S(1)} %copy-done.6, bf16[1536,512]{1,0:T(8,128)(2,1)S(1)} %copy-done.4, bf16[1536]{0:T(1024)(128)(2,1)S(1)} %get-tuple-element.419, ...), kind=kLoop, calls=%fused_computation.64 | loop fusion | flops 25165824 | bytes 9508864 | tf_op jit(solution)/shard_map/stack | solution.py:268
  424.0 6.5 fusion.23
  430.5 20.3 %fusion.80 = (bf16[1,1536,512]{2,1,0:T(8,128)(2,1)}, bf16[1,1536,512]{2,1,0:T(8,128)(2,1)}, bf16[1536,512]{1,0:T(8,128)(2,1)}, f32[1,1536,512]{2,1,0:T(8,128)}, ...) fusion(f32[1536,1024]{1,0:T(8,128)} %fusion.199, ...), kind=kOutput, calls=%fused_computation.131 | convolution fusion | flops 4887674880 | bytes 50350080 | tf_op jit(solution)/shard_map/dot_general | solution.py:276
  450.9 4.8 fusion.73
  455.7 3.1 add_bitcast_fusion
  459.0 3.0 fusion.74
  464.0 2.3 convolution_add_fusion.3
  466.4 7.8 fusion.55
  474.3 8.3 %convolution_add_fusion.2 = f32[1536,1024]{1,0:T(8,128)} fusion(f32[1536,1024]{1,0:T(8,128)S(1)} %fusion.55, bf16[1536,512]{1,0:T(8,128)(2,1)S(1)} %copy-done.7, bf16[1536,512]{1,0:T(8,128)(2,1)S(1)} %copy-done.5, bf16[1536,512]{1,0:T(8,128)(2,1)S(1)} %copy-done.29, bf16[1536,512]{1,0:T(8,128)(2,1)S(1)} %copy-done.15, bf16[1536,512]{1,0:T(8,128)(2,1)S(1)} %copy-done.28), kind=kOutput, calls=%fused_computation.37 | convolution fusion | flops 4853858304 | bytes 20447232 | tf_op jit(solution)/shard_map/dot_general | solution.py:40
  483.1 14.7 %reduce-scatter.15.cloned.1.call-done = f32[256,1024]{0,1:T(8,128)} async-done(((f32[512,1024]{0,1:T(8,128)}), f32[256,1024]{0,1:T(8,128)}) %reduce-scatter.15.cloned.1.call-update) | async-done | bytes 1048592 | tf_op jit(solution)/shard_map/reduce_scatter | solution.py:288
  497.8 34.6 %reduce-scatter.13.cloned.1.call-done = f32[256,1024]{1,0:T(8,128)} async-done(((f32[512,1024]{1,0:T(8,128)}), f32[256,1024]{1,0:T(8,128)}) %reduce-scatter.13.cloned.1.call-update) | async-done | bytes 1048592 | tf_op jit(solution)/shard_map/reduce_scatter | solution.py:287
  532.4 79.8 %reduce-scatter.17.cloned.1.call-done = f32[3,256,1024]{2,1,0:T(8,128)} async-done(((f32[3,512,1024]{2,1,0:T(8,128)}), f32[3,256,1024]{2,1,0:T(8,128)}) %reduce-scatter.17.cloned.1.call-update) | async-done | bytes 3145744 | tf_op jit(solution)/shard_map/reduce_scatter | solution.py:289
  614.9 3.2 fusion.197
  626.1 3.4 maximum_bitcast_fusion
  629.5 176.1 %all-reduce.7.cloned.1.call-done = (f32[256,1024]{1,0:T(8,128)}, f32[256,1024]{0,1:T(8,128)}, f32[3,256,1024]{2,1,0:T(8,128)}, f32[256,512]{0,1:T(8,128)}, f32[2...) async-done(((f32[256,1024]{1,0:T(8,128)}, f32[256,1024]{0,1:T(8,128)}, f32[3,256,1024]{2,1,0:T(8,128)}, ...) | async-done | bytes 9437200 | tf_op jit(solution)/shard_map/psum | solution.py:297
  811.8 2.5 copy.139
  814.4 2.3 copy.221
  (380 shorter events, 80.2 us)
Async XLA Ops:
  7.2 152.4 %all-gather.12.cloned.1.call-start = ((), (), s32[]{:S(2)}) async-start(), calls=%async_computation.11 | async-start | bytes 1572864 | tf_op jit(solution)/shard_map/all_gather | solution.py:127
  9.5 156.3 %all-gather.10.cloned.1.call-start = ((), (), s32[]{:S(2)}) async-start(), calls=%async_computation.10 | async-start | bytes 1572864 | tf_op jit(solution)/shard_map/all_gather | solution.py:126
  11.7 185.5 %all-gather.14.cloned.1.call-start = ((), (), s32[]{:S(2)}) async-start(), calls=%async_computation.12 | async-start | bytes 4718592 | tf_op jit(solution)/shard_map/all_gather | solution.py:128
  13.2 20.0 %copy-start.44 = (bf16[2,1,16,512]{3,2,1,0:T(8,128)(2,1)S(1)}, bf16[2,1,16,512]{3,2,1,0:T(8,128)(2,1)}, u32[]{:S(2)}) copy-start(bf16[2,1,16,512]{3,2,1,0:T(8,128)(2,1)} %param.25) | copy-start | bytes 98308
  13.2 193.3 %all-gather.18.cloned.1.call-start = ((), (), s32[]{:S(2)}) async-start(), calls=%async_computation.14 | async-start | bytes 1572864 | tf_op jit(solution)/shard_map/all_gather | solution.py:134
  15.4 18.7 %copy-start.46 = (f32[256,512]{1,0:T(8,128)S(1)}, f32[256,512]{1,0:T(8,128)}, u32[]{:S(2)}) copy-start(f32[256,512]{1,0:T(8,128)} %param.32) | copy-start | bytes 1572868
  15.4 241.4 %all-gather.16.cloned.1.call-start = ((), (), s32[]{:S(2)}) async-start(), calls=%async_computation.13 | async-start | bytes 1572864 | tf_op jit(solution)/shard_map/all_gather | solution.py:133
  16.4 29.0 %copy-start.62 = (s32[2,1,30]{2,1,0:T(1,128)S(1)}, s32[2,1,30]{2,1,0:T(1,128)}, u32[]{:S(2)}) copy-start(s32[2,1,30]{2,1,0:T(1,128)} %param.24) | copy-start | bytes 724
  16.4 29.1 %copy-start.52 = (f32[16,512]{1,0:T(8,128)S(1)}, f32[16,512]{1,0:T(8,128)}, u32[]{:S(2)}) copy-start(f32[16,512]{1,0:T(8,128)} %param.26) | copy-start | bytes 98308
  16.4 33.5 %copy-start.47 = (f32[256,512]{1,0:T(8,128)S(1)}, f32[256,512]{1,0:T(8,128)}, u32[]{:S(2)}) copy-start(f32[256,512]{1,0:T(8,128)} %param.30) | copy-start | bytes 1572868
  16.4 286.6 %reduce-scatter.11.cloned.1.call-start = ((), (), s32[]{:S(2)}) async-start(), calls=%async_computation.15 | async-start | bytes 98304 | tf_op jit(solution)/shard_map/reduce_scatter | solution.py:286
  17.4 149.9 %copy-start.53 = (s32[1536]{0:T(1024)}, s32[1536]{0:T(1024)S(1)}, u32[]{:S(2)}) copy-start(s32[1536]{0:T(1024)S(1)} %slice.240) | copy-start | bytes 18436
  34.2 108.2 %copy-start.48 = (f32[256,512]{1,0:T(8,128)S(1)}, f32[256,512]{1,0:T(8,128)}, u32[]{:S(2)}) copy-start(f32[256,512]{1,0:T(8,128)} %param.33) | copy-start | bytes 1572868
  45.4 112.0 %copy-start.50 = (f32[1536]{0:T(1024)}, f32[1536]{0:T(1024)S(1)}, u32[]{:S(2)}) copy-start(f32[1536]{0:T(1024)S(1)} %convert_element_type.345) | copy-start | bytes 18436
  180.8 9.1 %copy-start.16 = (bf16[1536,512]{1,0:T(8,128)(2,1)}, bf16[1536,512]{1,0:T(8,128)(2,1)S(1)}, u32[]{:S(2)}) copy-start(bf16[1536,512]{1,0:T(8,128)(2,1)S(1)} %get-tuple-element.405) | copy-start | bytes 4718596
  180.8 16.4 %copy-start.14 = (bf16[1536,512]{1,0:T(8,128)(2,1)}, bf16[1536,512]{1,0:T(8,128)(2,1)S(1)}, u32[]{:S(2)}) copy-start(bf16[1536,512]{1,0:T(8,128)(2,1)S(1)} %get-tuple-element.404) | copy-start | bytes 4718596
  180.8 9.1 %collective-permute-start.2 = (bf16[16,512]{1,0:T(8,128)(2,1)S(1)}, bf16[16,512]{1,0:T(8,128)(2,1)S(1)}, u32[]{:S(2)}, u32[]{:S(2)}) collective-permute-start(bf16[16,512]{1,0:T(8,128)(2,1)S(1)} %get-tuple-element.416), channel_id=1, source_target_pairs={{0,2},{2,4},{4,6},{6,8},{8,10},{10,12},{12,14},{14,16},{16,18},{18... | collective-permute-start | bytes 49160 | tf_op jit(solution)/shard_map/ppermute | solution.py:20
  182.1 7.8 collective-permute-start.3
  183.4 10.2 %collective-permute-start = (bf16[16,512]{1,0:T(8,128)(2,1)S(1)}, bf16[16,512]{1,0:T(8,128)(2,1)S(1)}, u32[]{:S(2)}, u32[]{:S(2)}) collective-permute-start(bf16[16,512]{1,0:T(8,128)(2,1)S(1)} %get-tuple-element.412), channel_id=1, source_target_pairs={{0,2},{2,4},{4,6},{6,8},{8,10},{10,12},{12,14},{14,16},{16,18},{18... | collective-permute-start | bytes 49160 | tf_op jit(solution)/shard_map/ppermute | solution.py:20
  188.5 5.1 collective-permute-start.1
  206.4 8.5 %copy-start.26 = (bf16[1536,512]{1,0:T(8,128)(2,1)S(1)}, bf16[1536,512]{1,0:T(8,128)(2,1)}, u32[]{:S(2)}) copy-start(bf16[1536,512]{1,0:T(8,128)(2,1)} %get-tuple-element.414) | copy-start | bytes 4718596
  206.4 8.5 %copy-start.27 = (bf16[1536,512]{1,0:T(8,128)(2,1)S(1)}, bf16[1536,512]{1,0:T(8,128)(2,1)}, u32[]{:S(2)}) copy-start(bf16[1536,512]{1,0:T(8,128)(2,1)} %get-tuple-element.415) | copy-start | bytes 4718596
  206.5 8.5 %copy-start.65 = (bf16[3,512,1024]{2,1,0:T(8,128)(2,1)S(1)}, bf16[3,512,1024]{2,1,0:T(8,128)(2,1)}, u32[]{:S(2)}) copy-start(bf16[3,512,1024]{2,1,0:T(8,128)(2,1)} %all-gather.14.cloned.1.call-done) | copy-start | bytes 9437188
  256.8 37.6 %copy-start.57 = (f32[1024]{0:T(1024)}, f32[1024]{0:T(1024)S(1)}, u32[]{:S(2)}) copy-start(f32[1024]{0:T(1024)S(1)} %get-tuple-element.358) | copy-start | bytes 12292
  296.0 187.0 %reduce-scatter.19.cloned.1.call-start = ((), (), s32[]{:S(2)}) async-start(), calls=%async_computation.19 | async-start | bytes 1572864 | tf_op jit(solution)/shard_map/reduce_scatter | solution.py:290
  297.7 185.3 %reduce-scatter.23.cloned.1.call-start = ((), (), s32[]{:S(2)}) async-start(), calls=%async_computation.21 | async-start | bytes 1572864 | tf_op jit(solution)/shard_map/reduce_scatter | solution.py:292
  299.9 183.1 %reduce-scatter.21.cloned.1.call-start = ((), (), s32[]{:S(2)}) async-start(), calls=%async_computation.20 | async-start | bytes 1572864 | tf_op jit(solution)/shard_map/reduce_scatter | solution.py:291
  300.8 65.6 %copy-start.2 = (bf16[512,1024]{1,0:T(8,128)(2,1)S(1)}, bf16[512,1024]{1,0:T(8,128)(2,1)}, u32[]{:S(2)}) copy-start(bf16[512,1024]{1,0:T(8,128)(2,1)} %all-gather.16.cloned.1.call-done) | copy-start | bytes 3145732
  302.2 180.9 %reduce-scatter.25.cloned.1.call-start = ((), (), s32[]{:S(2)}) async-start(), calls=%async_computation.22 | async-start | bytes 1572864 | tf_op jit(solution)/shard_map/reduce_scatter | solution.py:293
  367.9 115.2 %reduce-scatter.29.cloned.1.call-start = ((), (), s32[]{:S(2)}) async-start(), calls=%async_computation.24 | async-start | bytes 3145728 | tf_op jit(solution)/shard_map/reduce_scatter | solution.py:295
  385.7 97.4 %reduce-scatter.27.cloned.1.call-start = ((), (), s32[]{:S(2)}) async-start(), calls=%async_computation.23 | async-start | bytes 3145728 | tf_op jit(solution)/shard_map/reduce_scatter | solution.py:294
  385.8 10.2 %copy-start.56 = (f32[1024]{0:T(1024)S(1)}, f32[1024]{0:T(1024)}, u32[]{:S(2)}) copy-start(f32[1024]{0:T(1024)} %copy-done.55) | copy-start | bytes 12292
  385.8 10.2 %copy-start.58 = (f32[1024]{0:T(1024)S(1)}, f32[1024]{0:T(1024)}, u32[]{:S(2)}) copy-start(f32[1024]{0:T(1024)} %copy-done.57) | copy-start | bytes 12292
  385.8 10.2 %copy-start.59 = (f32[512]{0:T(512)S(1)}, f32[512]{0:T(512)}, u32[]{:S(2)}) copy-start(f32[512]{0:T(512)} %get-tuple-element.374) | copy-start | bytes 6148
  385.8 10.2 %copy-start.60 = (f32[512]{0:T(512)S(1)}, f32[512]{0:T(512)}, u32[]{:S(2)}) copy-start(f32[512]{0:T(512)} %get-tuple-element.372) | copy-start | bytes 6148
  386.7 28.2 %collective-permute-start.4 = (bf16[16,1024]{1,0:T(8,128)(2,1)S(1)}, bf16[16,1024]{1,0:T(8,128)(2,1)S(1)}, u32[]{:S(2)}, u32[]{:S(2)}) collective-permute-start(bf16[16,1024]{1,0:T(8,128)(2,1)S(1)} %get-tuple-element.398), channel_id=1, source_target_pairs={{2,0},{4,2},{6,4},{8,6},{10,8},{12,10},{14,12},{16,14},{18,16},{20... | collective-permute-start | bytes 98312 | tf_op jit(solution)/shard_map/ppermute | solution.py:23
  388.0 26.9 %collective-permute-start.5 = (bf16[16,1024]{1,0:T(8,128)(2,1)S(1)}, bf16[16,1024]{1,0:T(8,128)(2,1)S(1)}, u32[]{:S(2)}, u32[]{:S(2)}) collective-permute-start(bf16[16,1024]{1,0:T(8,128)(2,1)S(1)} %get-tuple-element.399), channel_id=1, source_target_pairs={{0,2},{2,4},{4,6},{6,8},{8,10},{10,12},{12,14},{14,16},{16,18},{18... | collective-permute-start | bytes 98312 | tf_op jit(solution)/shard_map/ppermute | solution.py:20
  391.6 12.5 %collective-permute-start.6 = (bf16[16,1024]{1,0:T(8,128)(2,1)}, bf16[16,1024]{1,0:T(8,128)(2,1)S(1)}, u32[]{:S(2)}, u32[]{:S(2)}) collective-permute-start(bf16[16,1024]{1,0:T(8,128)(2,1)} %get-tuple-element.402), channel_id=1, source_target_pairs={{2,0},{4,2},{6,4},{8,6},{10,8},{12,10},{14,12},{16,14},{18,16},{20... | collective-permute-start | bytes 98312 | tf_op jit(solution)/shard_map/ppermute | solution.py:23
  392.9 11.2 %collective-permute-start.7 = (bf16[16,1024]{1,0:T(8,128)(2,1)S(1)}, bf16[16,1024]{1,0:T(8,128)(2,1)S(1)}, u32[]{:S(2)}, u32[]{:S(2)}) collective-permute-start(bf16[16,1024]{1,0:T(8,128)(2,1)S(1)} %get-tuple-element.403), channel_id=1, source_target_pairs={{0,2},{2,4},{4,6},{6,8},{8,10},{10,12},{12,14},{14,16},{16,18},{18... | collective-permute-start | bytes 98312 | tf_op jit(solution)/shard_map/ppermute | solution.py:20
  397.7 100.1 %reduce-scatter.15.cloned.1.call-start = ((), (), s32[]{:S(2)}) async-start(), calls=%async_computation.17 | async-start | bytes 3145728 | tf_op jit(solution)/shard_map/reduce_scatter | solution.py:288
  404.1 10.8 %copy-start.4 = (bf16[1536,512]{1,0:T(8,128)(2,1)S(1)}, bf16[1536,512]{1,0:T(8,128)(2,1)}, u32[]{:S(2)}) copy-start(bf16[1536,512]{1,0:T(8,128)(2,1)} %get-tuple-element.380) | copy-start | bytes 4718596
  404.1 10.8 %copy-start.6 = (bf16[1536,512]{1,0:T(8,128)(2,1)S(1)}, bf16[1536,512]{1,0:T(8,128)(2,1)}, u32[]{:S(2)}) copy-start(bf16[1536,512]{1,0:T(8,128)(2,1)} %get-tuple-element.381) | copy-start | bytes 4718596
  414.8 9.2 %copy-start.66 = (bf16[3,512,1024]{2,1,0:T(8,128)(2,1)S(1)}, bf16[3,512,1024]{2,1,0:T(8,128)(2,1)}, u32[]{:S(2)}) copy-start(bf16[3,512,1024]{2,1,0:T(8,128)(2,1)} %all-gather.14.cloned.1.call-done) | copy-start | bytes 9437188
  414.9 15.6 %slice-start = ((s8[6291456]{0:T(1024)(128)(4,1)}), s8[4194304]{0:T(1024)(128)(4,1)S(1)}, s32[]{:S(2)}) async-start(s8[6291456]{0:T(1024)(128)(4,1)} %bitcast.252), calls=%async_computation.26 | async-start | bytes 8388608
  458.9 73.5 %reduce-scatter.13.cloned.1.call-start = ((), (), s32[]{:S(2)}) async-start(), calls=%async_computation.16 | async-start | bytes 3145728 | tf_op jit(solution)/shard_map/reduce_scatter | solution.py:287
  466.3 145.9 %reduce-scatter.17.cloned.1.call-start = ((), (), s32[]{:S(2)}) async-start(), calls=%async_computation.18 | async-start | bytes 9437184 | tf_op jit(solution)/shard_map/reduce_scatter | solution.py:289
  482.7 322.9 %all-reduce.7.cloned.1.call-start = ((), (), s32[]{:S(2)}) async-start(), calls=%async_computation.25 | async-start | bytes 18874368 | tf_op jit(solution)/shard_map/psum | solution.py:297
  807.6 9.1 %copy-start.22 = (f32[3,256,1024]{2,1,0:T(8,128)S(1)}, f32[3,256,1024]{2,1,0:T(8,128)}, u32[]{:S(2)}) copy-start(f32[3,256,1024]{2,1,0:T(8,128)} %get-tuple-element.573) | copy-start | bytes 9437188
  (53 other events, 214.5 us)
Sparse Core Ops, SparseCore 0:
  10.1 30.0 all-gather.11
  42.4 26.2 all-gather.9
  70.7 45.4 all-gather.13
  118.2 21.2 all-gather.17
  141.5 22.1 all-gather.15
  296.2 6.0 reduce-scatter.10
  305.1 20.3 reduce-scatter.18
  328.3 20.3 reduce-scatter.22
  351.5 20.3 reduce-scatter.20
  374.6 20.3 reduce-scatter.24
  397.2 31.8 reduce-scatter.28
  431.3 31.8 reduce-scatter.26
  465.9 31.8 reduce-scatter.14
  500.6 31.8 reduce-scatter.12
  535.1 77.0 reduce-scatter.16
  617.6 187.9 all-reduce.6
where the time goes:
time: 832 us; the launch traced here: 828 us
  waiting for transfers between devices  306 us (37%)
  blocking collectives  256 us (31%)
  matrix products  135 us (16%)
  other arithmetic  69.2 us (8%)
  local copies, waits for them, and re-layouts  27.7 us (3%)
  starting transfers between devices  18.6 us (2%)
  between operations  15.6 us (2%)
    psum x1, waiting for transfers between devices, per_device(): lax.psum((shares[0], shares[1], shares[2], shares[3], shares[4], shares[5...  176 us
    reduce_scatter x1, waiting for transfers between devices, per_device(): lax.psum_scatter(acc_conv_taps, 'fsdp', scatter_dimension=1, tiled=True)  79.8 us
    all_gather x4, blocking collectives, joined_2(): gathered = jax.tree.map(lambda a: lax.all_gather(a, axis), part)  76.7 us
    psum x1, blocking collectives, per_device(): context = lax.psum(context_part, 'tm')  61.7 us
    dot_general x16, matrix products, contract_rows(): lax.dot_general(left, right, (((0,), (0,)), ((), ())), precision=precisio...  41.8 us
    reduce_scatter x1, waiting for transfers between devices, per_device(): lax.psum_scatter(acc_step, 'fsdp', scatter_dimension=0, tiled=True)  34.6 us
    psum x1, blocking collectives, per_device(): film_cot = lax.psum(film_local, 'tm')  32.8 us
    psum x1, blocking collectives, per_device(): row_total = lax.psum(row_part, 'tm')  30 us
  transfers between devices with their start and end apart: 24, of which 4 were waited for; matrix products, arithmetic and copies ran while one was open for 24% of the time, Pallas kernels for 0%

commit v1 on v0

--- a/solution.py
+++ b/solution.py
@@ -231,7 +231,11 @@
             "qhd,khd->hqk", context_cot_heads, value_heads, preferred_element_type=f32
         )
         row_part = jnp.sum(probs * prob_cot, axis=-1)
-        row_total = lax.psum(row_part, "tm")
+        row_total = row_part
+        for hop in (1, 2, 4, 8):
+            row_total = row_total + lax.ppermute(
+                row_total, "tm", [(dev, dev ^ hop) for dev in range(16)]
+            )
         score_cot = (probs * (prob_cot - row_total[..., None])).astype(bf16)
         query_cot = (
             jnp.einsum("hqk,khd->qhd", score_cot, key_heads, preferred_element_type=f32)

time: 832 us -> 816 us (0.981)
  blocking collectives: 256 us -> 227 us
    psum x1 -> x0, blocking collectives: 30 us -> none  [per_device(): row_total = lax.psum(row_part, 'tm')]
  transfers between devices with their start and end apart: 24 -> 32, of which waited for: 4 -> 12; matrix products, arithmetic and copies ran while one was open for 24% -> 24% of each run, Pallas kernels for 0% -> 0%
where the time goes in v1:
time: 816 us; the launch traced here: 812 us
  waiting for transfers between devices  312 us (38%)
  blocking collectives  227 us (28%)
  matrix products  135 us (17%)
  other arithmetic  69.1 us (8%)
  local copies, waits for them, and re-layouts  27.7 us (3%)
  starting transfers between devices  26.3 us (3%)
  between operations  15.6 us (2%)
    psum x1, waiting for transfers between devices, per_device(): lax.psum((shares[0], shares[1], shares[2], shares[3], shares[4], shares[5...  176 us
    reduce_scatter x1, waiting for transfers between devices, per_device(): lax.psum_scatter(acc_conv_taps, 'fsdp', scatter_dimension=1, tiled=True)  79.8 us
    all_gather x4, blocking collectives, joined_2(): gathered = jax.tree.map(lambda a: lax.all_gather(a, axis), part)  76.7 us
    psum x1, blocking collectives, per_device(): context = lax.psum(context_part, 'tm')  62.5 us
    dot_general x16, matrix products, contract_rows(): lax.dot_general(left, right, (((0,), (0,)), ((), ())), precision=precisio...  41.8 us
    reduce_scatter x1, waiting for transfers between devices, per_device(): lax.psum_scatter(acc_step, 'fsdp', scatter_dimension=0, tiled=True)  34.6 us
    psum x1, blocking collectives, per_device(): film_cot = lax.psum(film_local, 'tm')  32.8 us
    dot_general x2, matrix products, per_device(): lax.dot_general(back_taps, full_conv, (((1, 2), (0, 2)), ((), ())), prefe...  26.9 us
  transfers between devices with their start and end apart: 32, of which 12 were waited for; matrix products, arithmetic and copies ran while one was open for 24% of the time, Pallas kernels for 0%

profile of v1, /device:TPU:0, one launch (start us, length us, event | category | flops | bytes accessed | tf_op | source)
XLA Modules:
  0.0 812.4 jit_solution(11333347762466838583)
XLA Ops:
  7.2 2.2 convert_element_type.310
  17.6 15.5 %all_gather.70 = bf16[512,512]{1,0:T(8,128)(2,1)S(1)} all-gather(bf16[256,512]{1,0:T(8,128)(2,1)S(1)} %convert_element_type.320), channel_id=1, replica_groups=mesh['tm'=16,'fsdp'=2] {'fsdp'}, dimensions={0}, use_global_device_ids=true | all-gather | bytes 786432 | tf_op jit(solution)/shard_map/all_gather | solution.py:130
  34.2 10.2 %all_gather.67 = bf16[512,512]{1,0:T(8,128)(2,1)S(1)} all-gather(bf16[256,512]{1,0:T(8,128)(2,1)S(1)} %convert_element_type.315), channel_id=1, replica_groups=mesh['tm'=16,'fsdp'=2] {'fsdp'}, dimensions={0}, use_global_device_ids=true | all-gather | bytes 786432 | tf_op jit(solution)/shard_map/all_gather | solution.py:131
  45.4 4.4 all_gather.68
  49.9 13.5 %all_gather.69 = bf16[512,512]{1,0:T(8,128)(2,1)S(1)} all-gather(bf16[256,512]{1,0:T(8,128)(2,1)S(1)} %convert_element_type.318), channel_id=1, replica_groups=mesh['tm'=16,'fsdp'=2] {'fsdp'}, dimensions={0}, use_global_device_ids=true | all-gather | bytes 786432 | tf_op jit(solution)/shard_map/all_gather | solution.py:129
  64.0 22.6 %all-gather = f32[128,32]{1,0:T(8,128)S(1)} all-gather(f32[8,32]{1,0:T(8,128)S(1)} %get-tuple-element.436), channel_id=2, replica_groups=mesh['tm'=16,'fsdp'=2] {'tm'}, dimensions={0}, use_global_device_ids=true | all-gather | bytes 17408 | tf_op jit(solution)/shard_map/all_gather | solution.py:29
  86.6 17.6 %all-gather.1 = f32[128,32]{1,0:T(8,128)S(1)} all-gather(f32[8,32]{1,0:T(8,128)S(1)} %exponential_reduce_fusion.1), channel_id=3, replica_groups=mesh['tm'=16,'fsdp'=2] {'tm'}, dimensions={0}, use_global_device_ids=true | all-gather | bytes 17408 | tf_op jit(solution)/shard_map/all_gather | solution.py:29
  105.0 18.9 %all-gather.2 = f32[128,32]{1,0:T(8,128)S(1)} all-gather(f32[8,32]{1,0:T(8,128)S(1)} %get-tuple-element.434), channel_id=4, replica_groups=mesh['tm'=16,'fsdp'=2] {'tm'}, dimensions={0}, use_global_device_ids=true | all-gather | bytes 17408 | tf_op jit(solution)/shard_map/all_gather | solution.py:29
  124.0 17.6 %all-gather.3 = f32[128,32]{1,0:T(8,128)S(1)} all-gather(f32[8,32]{1,0:T(8,128)S(1)} %exponential_reduce_fusion), channel_id=5, replica_groups=mesh['tm'=16,'fsdp'=2] {'tm'}, dimensions={0}, use_global_device_ids=true | all-gather | bytes 17408 | tf_op jit(solution)/shard_map/all_gather | solution.py:29
  142.4 11.0 %all_gather.75 = bf16[512,512]{1,0:T(8,128)(2,1)S(1)} all-gather(bf16[256,512]{1,0:T(8,128)(2,1)S(1)} %convert_element_type.324), channel_id=1, replica_groups=mesh['tm'=16,'fsdp'=2] {'fsdp'}, dimensions={0}, use_global_device_ids=true | all-gather | bytes 786432 | tf_op jit(solution)/shard_map/all_gather | solution.py:132
  153.8 3.6 fusion.63
  159.5 6.2 fusion.88
  167.2 5.3 convolution_add_fusion
  174.9 2.9 convolution_add_fusion.1
  183.3 5.1 collective-permute-start
  189.8 3.7 fusion.84
  193.5 3.5 fusion.86
  197.1 9.3 %fusion.78 = f32[1536,1024]{1,0:T(8,128)} fusion(bf16[1536,1024]{1,0:T(8,128)(2,1)} %bitcast.275, bf16[1536,512]{1,0:T(8,128)(2,1)} %get-tuple-element.409, bf16[1536,512]{1,0:T(8,128)(2,1)S(1)} %get-tuple-element.402, bf16[1536,512]{1,0:T(8,128)(2,1)} %get-tuple-element.408), kind=kOutput, calls=%fused_computation.128 | convolution fusion | flops 4845993984 | bytes 14155776 | tf_op jit(solution)/shard_map/dot_general | solution.py:178
  206.3 8.5 %multiply_reduce_fusion.1 = (f32[512]{0:T(512)S(1)}, f32[512]{0:T(512)S(1)}, f32[1536,512]{1,0:T(8,128)}) fusion(f32[1536,1024]{1,0:T(8,128)} %fusion.78, bf16[512,1024]{1,0:T(8,128)(2,1)} %all-gather.18.cloned.1.call-done, bf16[1536,512]{1,0:T(8,128)(2,1)} %get-tuple-element.406, bf16[1536,512]{1,0:T(8,128)(2,1)} %get-tuple-element.404), kind=kOutput, calls=%fused_computation.108 | convolution fusion | flops 1622408192 | bytes 13635584 | tf_op jit(solution)/shard_map/dot_general | solution.py:50
  214.9 5.1 fusion.77
  220.0 3.9 multiply_reduce_fusion
  223.9 32.8 %all-reduce.1 = (f32[1024]{0:T(1024)S(1)}, f32[1024]{0:T(1024)S(1)}) all-reduce(f32[1024]{0:T(1024)S(1)} %pad_maximum_fusion.45, f32[1024]{0:T(1024)S(1)} %pad_maximum_fusion.44), channel_id=1, replica_groups=mesh['tm'=16,'fsdp'=2] {'tm'}, use_global_device_ids=true, to_apply=%region_22.23 | all-reduce | flops 2048 | bytes 16384 | tf_op jit(solution)/shard_map/psum | solution.py:221
  271.3 2.9 collective-permute-start.11
  286.7 62.5 %all-reduce.7 = (bf16[32,512]{1,0:T(8,128)(2,1)S(1)}, bf16[32,512]{1,0:T(8,128)(2,1)S(1)}, f32[16,512]{1,0:T(8,128)}) all-reduce(f32[32,512]{1,0:T(8,128)S(1)} %reshape.308, f32[32,512]{1,0:T(8,128)S(1)} %reshape.303, f32[16,512]{1,0:T(8,128)} %reduce-scatter.11.cloned.1.call-done), channel_id=1, replica_groups=mesh['tm'=16,'fsdp'=2] {'tm'}, use_global_device_ids=true, to_apply=%region_14.15 | all-reduce | flops 40960 | bytes 262144 | tf_op jit(solution)/shard_map/psum | solution.py:201
  352.5 5.8 multiply_convert_fusion.1
  362.6 3.2 multiply_convert_fusion.3
  367.0 3.1 fusion.95
  372.7 3.0 collective-permute-start.5
  377.7 3.0 collective-permute-start.7
  382.6 6.3 fusion.199
  388.9 10.6 %fusion.39 = (bf16[1536,1,1024]{2,0,1:T(8,128)(2,1)}, bf16[1536,1,1024]{2,0,1:T(8,128)(2,1)}) fusion(bf16[16,1024]{1,0:T(8,128)(2,1)S(1)} %collective-permute-done.6, bf16[1536,512]{1,0:T(8,128)(2,1)S(1)} %copy-done.3, bf16[1536,512]{1,0:T(8,128)(2,1)S(1)} %get-tuple-element.380, bf16[1536]{0:T(1024)(128)(2,1)S(1)} %get-tuple-element.419, ...), kind=kLoop, calls=%fused_computation.56 | loop fusion | flops 25165824 | bytes 9508864 | tf_op jit(solution)/shard_map/stack | solution.py:272
  399.5 9.1 %fusion.43 = (bf16[1536,1,1024]{2,0,1:T(8,128)(2,1)S(1)}, bf16[1536,1,1024]{2,0,1:T(8,128)(2,1)S(1)}) fusion(bf16[16,1024]{1,0:T(8,128)(2,1)S(1)} %collective-permute-done.4, bf16[1536,512]{1,0:T(8,128)(2,1)S(1)} %copy-done.6, bf16[1536,512]{1,0:T(8,128)(2,1)S(1)} %copy-done.4, bf16[1536]{0:T(1024)(128)(2,1)S(1)} %get-tuple-element.417, ...), kind=kLoop, calls=%fused_computation.64 | loop fusion | flops 25165824 | bytes 9508864 | tf_op jit(solution)/shard_map/stack | solution.py:272
  408.6 6.5 fusion.23
  415.1 20.4 %fusion.80 = (bf16[1,1536,512]{2,1,0:T(8,128)(2,1)}, bf16[1,1536,512]{2,1,0:T(8,128)(2,1)}, bf16[1536,512]{1,0:T(8,128)(2,1)}, f32[1,1536,512]{2,1,0:T(8,128)}, ...) fusion(f32[1536,1024]{1,0:T(8,128)} %fusion.199, ...), kind=kOutput, calls=%fused_computation.131 | convolution fusion | flops 4887674880 | bytes 50350080 | tf_op jit(solution)/shard_map/dot_general | solution.py:280
  435.5 4.8 fusion.73
  440.4 3.1 add_bitcast_fusion
  443.6 3.0 fusion.74
  448.6 2.3 convolution_add_fusion.3
  451.1 7.8 fusion.55
  459.0 8.3 %convolution_add_fusion.2 = f32[1536,1024]{1,0:T(8,128)} fusion(f32[1536,1024]{1,0:T(8,128)S(1)} %fusion.55, bf16[1536,512]{1,0:T(8,128)(2,1)S(1)} %copy-done.7, bf16[1536,512]{1,0:T(8,128)(2,1)S(1)} %copy-done.5, bf16[1536,512]{1,0:T(8,128)(2,1)S(1)} %copy-done.29, bf16[1536,512]{1,0:T(8,128)(2,1)S(1)} %copy-done.15, bf16[1536,512]{1,0:T(8,128)(2,1)S(1)} %copy-done.28), kind=kOutput, calls=%fused_computation.37 | convolution fusion | flops 4853858304 | bytes 20447232 | tf_op jit(solution)/shard_map/dot_general | solution.py:40
  467.8 14.5 %reduce-scatter.15.cloned.1.call-done = f32[256,1024]{0,1:T(8,128)} async-done(((f32[512,1024]{0,1:T(8,128)}), f32[256,1024]{0,1:T(8,128)}) %reduce-scatter.15.cloned.1.call-update) | async-done | bytes 1048592 | tf_op jit(solution)/shard_map/reduce_scatter | solution.py:292
  482.3 34.6 %reduce-scatter.13.cloned.1.call-done = f32[256,1024]{1,0:T(8,128)} async-done(((f32[512,1024]{1,0:T(8,128)}), f32[256,1024]{1,0:T(8,128)}) %reduce-scatter.13.cloned.1.call-update) | async-done | bytes 1048592 | tf_op jit(solution)/shard_map/reduce_scatter | solution.py:291
  516.9 79.8 %reduce-scatter.17.cloned.1.call-done = f32[3,256,1024]{2,1,0:T(8,128)} async-done(((f32[3,512,1024]{2,1,0:T(8,128)}), f32[3,256,1024]{2,1,0:T(8,128)}) %reduce-scatter.17.cloned.1.call-update) | async-done | bytes 3145744 | tf_op jit(solution)/shard_map/reduce_scatter | solution.py:293
  599.4 3.2 fusion.197
  610.6 3.4 maximum_bitcast_fusion
  614.0 176.1 %all-reduce.6.cloned.1.call-done = (f32[256,1024]{1,0:T(8,128)}, f32[256,1024]{0,1:T(8,128)}, f32[3,256,1024]{2,1,0:T(8,128)}, f32[256,512]{0,1:T(8,128)}, f32[2...) async-done(((f32[256,1024]{1,0:T(8,128)}, f32[256,1024]{0,1:T(8,128)}, f32[3,256,1024]{2,1,0:T(8,128)}, ...) | async-done | bytes 9437200 | tf_op jit(solution)/shard_map/psum | solution.py:301
  796.3 2.5 copy.139
  798.8 2.3 copy.221
  (403 shorter events, 91.3 us)
Async XLA Ops:
  7.2 152.3 %all-gather.12.cloned.1.call-start = ((), (), s32[]{:S(2)}) async-start(), calls=%async_computation.11 | async-start | bytes 1572864 | tf_op jit(solution)/shard_map/all_gather | solution.py:127
  9.5 156.2 %all-gather.10.cloned.1.call-start = ((), (), s32[]{:S(2)}) async-start(), calls=%async_computation.10 | async-start | bytes 1572864 | tf_op jit(solution)/shard_map/all_gather | solution.py:126
  11.7 185.4 %all-gather.14.cloned.1.call-start = ((), (), s32[]{:S(2)}) async-start(), calls=%async_computation.12 | async-start | bytes 4718592 | tf_op jit(solution)/shard_map/all_gather | solution.py:128
  13.2 20.0 %copy-start.44 = (bf16[2,1,16,512]{3,2,1,0:T(8,128)(2,1)S(1)}, bf16[2,1,16,512]{3,2,1,0:T(8,128)(2,1)}, u32[]{:S(2)}) copy-start(bf16[2,1,16,512]{3,2,1,0:T(8,128)(2,1)} %param.25) | copy-start | bytes 98308
  13.2 193.2 %all-gather.18.cloned.1.call-start = ((), (), s32[]{:S(2)}) async-start(), calls=%async_computation.14 | async-start | bytes 1572864 | tf_op jit(solution)/shard_map/all_gather | solution.py:134
  15.4 18.7 %copy-start.46 = (f32[256,512]{1,0:T(8,128)S(1)}, f32[256,512]{1,0:T(8,128)}, u32[]{:S(2)}) copy-start(f32[256,512]{1,0:T(8,128)} %param.32) | copy-start | bytes 1572868
  15.4 241.3 %all-gather.16.cloned.1.call-start = ((), (), s32[]{:S(2)}) async-start(), calls=%async_computation.13 | async-start | bytes 1572864 | tf_op jit(solution)/shard_map/all_gather | solution.py:133
  16.4 29.0 %copy-start.62 = (s32[2,1,30]{2,1,0:T(1,128)S(1)}, s32[2,1,30]{2,1,0:T(1,128)}, u32[]{:S(2)}) copy-start(s32[2,1,30]{2,1,0:T(1,128)} %param.24) | copy-start | bytes 724
  16.4 29.0 %copy-start.52 = (f32[16,512]{1,0:T(8,128)S(1)}, f32[16,512]{1,0:T(8,128)}, u32[]{:S(2)}) copy-start(f32[16,512]{1,0:T(8,128)} %param.26) | copy-start | bytes 98308
  16.4 33.5 %copy-start.47 = (f32[256,512]{1,0:T(8,128)S(1)}, f32[256,512]{1,0:T(8,128)}, u32[]{:S(2)}) copy-start(f32[256,512]{1,0:T(8,128)} %param.30) | copy-start | bytes 1572868
  16.4 270.3 %reduce-scatter.11.cloned.1.call-start = ((), (), s32[]{:S(2)}) async-start(), calls=%async_computation.15 | async-start | bytes 98304 | tf_op jit(solution)/shard_map/reduce_scatter | solution.py:290
  17.4 149.8 %copy-start.53 = (s32[1536]{0:T(1024)}, s32[1536]{0:T(1024)S(1)}, u32[]{:S(2)}) copy-start(s32[1536]{0:T(1024)S(1)} %slice.240) | copy-start | bytes 18436
  34.2 108.2 %copy-start.48 = (f32[256,512]{1,0:T(8,128)S(1)}, f32[256,512]{1,0:T(8,128)}, u32[]{:S(2)}) copy-start(f32[256,512]{1,0:T(8,128)} %param.33) | copy-start | bytes 1572868
  45.4 112.0 %copy-start.50 = (f32[1536]{0:T(1024)}, f32[1536]{0:T(1024)S(1)}, u32[]{:S(2)}) copy-start(f32[1536]{0:T(1024)S(1)} %convert_element_type.345) | copy-start | bytes 18436
  180.7 16.4 %copy-start.14 = (bf16[1536,512]{1,0:T(8,128)(2,1)}, bf16[1536,512]{1,0:T(8,128)(2,1)S(1)}, u32[]{:S(2)}) copy-start(bf16[1536,512]{1,0:T(8,128)(2,1)S(1)} %get-tuple-element.402) | copy-start | bytes 4718596
  180.7 9.1 %collective-permute-start.2 = (bf16[16,512]{1,0:T(8,128)(2,1)S(1)}, bf16[16,512]{1,0:T(8,128)(2,1)S(1)}, u32[]{:S(2)}, u32[]{:S(2)}) collective-permute-start(bf16[16,512]{1,0:T(8,128)(2,1)S(1)} %get-tuple-element.414), channel_id=1, source_target_pairs={{0,2},{2,4},{4,6},{6,8},{8,10},{10,12},{12,14},{14,16},{16,18},{18... | collective-permute-start | bytes 49160 | tf_op jit(solution)/shard_map/ppermute | solution.py:20
  182.0 7.8 collective-permute-start.3
  183.3 10.2 %collective-permute-start = (bf16[16,512]{1,0:T(8,128)(2,1)S(1)}, bf16[16,512]{1,0:T(8,128)(2,1)S(1)}, u32[]{:S(2)}, u32[]{:S(2)}) collective-permute-start(bf16[16,512]{1,0:T(8,128)(2,1)S(1)} %get-tuple-element.410), channel_id=1, source_target_pairs={{0,2},{2,4},{4,6},{6,8},{8,10},{10,12},{12,14},{14,16},{16,18},{18... | collective-permute-start | bytes 49160 | tf_op jit(solution)/shard_map/ppermute | solution.py:20
  188.5 5.1 collective-permute-start.1
  262.5 1.2 collective-permute-start.12
  262.7 1.4 collective-permute-start.8
  263.7 3.6 collective-permute-start.13
  264.1 3.6 collective-permute-start.9
  267.3 3.6 collective-permute-start.14
  267.7 3.6 collective-permute-start.10
  270.9 4.5 collective-permute-start.15
  271.3 4.5 collective-permute-start.11
  278.1 189.6 %reduce-scatter.23.cloned.1.call-start = ((), (), s32[]{:S(2)}) async-start(), calls=%async_computation.21 | async-start | bytes 1572864 | tf_op jit(solution)/shard_map/reduce_scatter | solution.py:296
  279.4 188.2 %reduce-scatter.19.cloned.1.call-start = ((), (), s32[]{:S(2)}) async-start(), calls=%async_computation.19 | async-start | bytes 1572864 | tf_op jit(solution)/shard_map/reduce_scatter | solution.py:294
  281.8 185.9 %reduce-scatter.21.cloned.1.call-start = ((), (), s32[]{:S(2)}) async-start(), calls=%async_computation.20 | async-start | bytes 1572864 | tf_op jit(solution)/shard_map/reduce_scatter | solution.py:295
  282.7 68.2 %copy-start.2 = (bf16[512,1024]{1,0:T(8,128)(2,1)S(1)}, bf16[512,1024]{1,0:T(8,128)(2,1)}, u32[]{:S(2)}) copy-start(bf16[512,1024]{1,0:T(8,128)(2,1)} %all-gather.16.cloned.1.call-done) | copy-start | bytes 3145732
  284.0 183.7 %reduce-scatter.25.cloned.1.call-start = ((), (), s32[]{:S(2)}) async-start(), calls=%async_computation.22 | async-start | bytes 1572864 | tf_op jit(solution)/shard_map/reduce_scatter | solution.py:297
  352.4 115.4 %reduce-scatter.29.cloned.1.call-start = ((), (), s32[]{:S(2)}) async-start(), calls=%async_computation.24 | async-start | bytes 3145728 | tf_op jit(solution)/shard_map/reduce_scatter | solution.py:299
  370.2 97.6 %reduce-scatter.27.cloned.1.call-start = ((), (), s32[]{:S(2)}) async-start(), calls=%async_computation.23 | async-start | bytes 3145728 | tf_op jit(solution)/shard_map/reduce_scatter | solution.py:298
  370.4 10.3 %copy-start.56 = (f32[1024]{0:T(1024)S(1)}, f32[1024]{0:T(1024)}, u32[]{:S(2)}) copy-start(f32[1024]{0:T(1024)} %copy-done.55) | copy-start | bytes 12292
  370.4 10.3 %copy-start.58 = (f32[1024]{0:T(1024)S(1)}, f32[1024]{0:T(1024)}, u32[]{:S(2)}) copy-start(f32[1024]{0:T(1024)} %copy-done.57) | copy-start | bytes 12292
  370.4 10.3 %copy-start.59 = (f32[512]{0:T(512)S(1)}, f32[512]{0:T(512)}, u32[]{:S(2)}) copy-start(f32[512]{0:T(512)} %get-tuple-element.372) | copy-start | bytes 6148
  371.4 28.0 %collective-permute-start.4 = (bf16[16,1024]{1,0:T(8,128)(2,1)S(1)}, bf16[16,1024]{1,0:T(8,128)(2,1)S(1)}, u32[]{:S(2)}, u32[]{:S(2)}) collective-permute-start(bf16[16,1024]{1,0:T(8,128)(2,1)S(1)} %get-tuple-element.396), channel_id=1, source_target_pairs={{2,0},{4,2},{6,4},{8,6},{10,8},{12,10},{14,12},{16,14},{18,16},{20... | collective-permute-start | bytes 98312 | tf_op jit(solution)/shard_map/ppermute | solution.py:23
  372.7 26.8 %collective-permute-start.5 = (bf16[16,1024]{1,0:T(8,128)(2,1)S(1)}, bf16[16,1024]{1,0:T(8,128)(2,1)S(1)}, u32[]{:S(2)}, u32[]{:S(2)}) collective-permute-start(bf16[16,1024]{1,0:T(8,128)(2,1)S(1)} %get-tuple-element.397), channel_id=1, source_target_pairs={{0,2},{2,4},{4,6},{6,8},{8,10},{10,12},{12,14},{14,16},{16,18},{18... | collective-permute-start | bytes 98312 | tf_op jit(solution)/shard_map/ppermute | solution.py:20
  376.4 12.5 %collective-permute-start.6 = (bf16[16,1024]{1,0:T(8,128)(2,1)}, bf16[16,1024]{1,0:T(8,128)(2,1)S(1)}, u32[]{:S(2)}, u32[]{:S(2)}) collective-permute-start(bf16[16,1024]{1,0:T(8,128)(2,1)} %get-tuple-element.400), channel_id=1, source_target_pairs={{2,0},{4,2},{6,4},{8,6},{10,8},{12,10},{14,12},{16,14},{18,16},{20... | collective-permute-start | bytes 98312 | tf_op jit(solution)/shard_map/ppermute | solution.py:23
  377.7 11.2 %collective-permute-start.7 = (bf16[16,1024]{1,0:T(8,128)(2,1)S(1)}, bf16[16,1024]{1,0:T(8,128)(2,1)S(1)}, u32[]{:S(2)}, u32[]{:S(2)}) collective-permute-start(bf16[16,1024]{1,0:T(8,128)(2,1)S(1)} %get-tuple-element.401), channel_id=1, source_target_pairs={{0,2},{2,4},{4,6},{6,8},{8,10},{10,12},{12,14},{14,16},{16,18},{18... | collective-permute-start | bytes 98312 | tf_op jit(solution)/shard_map/ppermute | solution.py:20
  382.5 99.8 %reduce-scatter.15.cloned.1.call-start = ((), (), s32[]{:S(2)}) async-start(), calls=%async_computation.17 | async-start | bytes 3145728 | tf_op jit(solution)/shard_map/reduce_scatter | solution.py:292
  388.8 10.6 %copy-start.4 = (bf16[1536,512]{1,0:T(8,128)(2,1)S(1)}, bf16[1536,512]{1,0:T(8,128)(2,1)}, u32[]{:S(2)}) copy-start(bf16[1536,512]{1,0:T(8,128)(2,1)} %get-tuple-element.378) | copy-start | bytes 4718596
  388.9 10.6 %copy-start.6 = (bf16[1536,512]{1,0:T(8,128)(2,1)S(1)}, bf16[1536,512]{1,0:T(8,128)(2,1)}, u32[]{:S(2)}) copy-start(bf16[1536,512]{1,0:T(8,128)(2,1)} %get-tuple-element.379) | copy-start | bytes 4718596
  399.5 15.6 %slice-start = ((s8[6291456]{0:T(1024)(128)(4,1)}), s8[4194304]{0:T(1024)(128)(4,1)S(1)}, s32[]{:S(2)}) async-start(s8[6291456]{0:T(1024)(128)(4,1)} %bitcast.252), calls=%async_computation.26 | async-start | bytes 8388608
  443.5 73.3 %reduce-scatter.13.cloned.1.call-start = ((), (), s32[]{:S(2)}) async-start(), calls=%async_computation.16 | async-start | bytes 3145728 | tf_op jit(solution)/shard_map/reduce_scatter | solution.py:291
  451.0 145.7 %reduce-scatter.17.cloned.1.call-start = ((), (), s32[]{:S(2)}) async-start(), calls=%async_computation.18 | async-start | bytes 9437184 | tf_op jit(solution)/shard_map/reduce_scatter | solution.py:293
  467.3 322.7 %all-reduce.6.cloned.1.call-start = ((), (), s32[]{:S(2)}) async-start(), calls=%async_computation.25 | async-start | bytes 18874368 | tf_op jit(solution)/shard_map/psum | solution.py:301
  (61 other events, 280.0 us)
Sparse Core Ops, SparseCore 0:
  10.1 30.0 all-gather.11
  42.4 26.1 all-gather.9
  70.7 45.4 all-gather.13
  118.2 21.2 all-gather.17
  141.5 22.1 all-gather.15
  278.2 8.4 reduce-scatter.10
  289.5 20.2 reduce-scatter.22
  312.8 20.3 reduce-scatter.18
  335.9 20.3 reduce-scatter.20
  359.1 20.3 reduce-scatter.24
  381.6 31.8 reduce-scatter.28
  415.7 31.8 reduce-scatter.26
  450.4 31.8 reduce-scatter.14
  485.0 31.8 reduce-scatter.12
  519.6 77.0 reduce-scatter.16
  602.0 187.9 all-reduce.5
